TPU v7x, 32 devices: a whole 2x2x4 slice. The times are simulated.
32 devices in a mesh: grid: 4 (over y, x), row: 4 (over z), rhs: 2 (over core).
Axes of the slice: x: 2, y: 2, z: 4, core: 2. Of those that a mesh axis runs over, the one named last changes fastest.
Arguments:
- leaf_rhs: float32 [12288, 2048], P(('grid', 'row'), 'rhs'), parts along dimension 1, may hold values from -6 to 6
- block_sizes: int32 [16], P(('grid', 'row')), may hold values from 384 to 768, as said below
- leaf_lower: float32 [12288, 256], P(('grid', 'row')), may hold values from -0.25 to 0.25
- leaf_inverse: float32 [12288, 768], P(('grid', 'row')), as said below
- coupling: float32 [8192, 768], P(('grid', 'row')), may hold values from -0.0546875 to 0.0546875
- anc_rows: int32 [8192], P(('grid', 'row')), may hold values from 0 to 767, as said below
- anc_rhs: float32 [768, 2048], P(None, 'rhs'), parts along dimension 1, may hold values from -6 to 6
- anc_inverse: float32 [768, 768], replicated, as said below
Outputs:
- leaf_solution: float32 [12288, 2048], P(('grid', 'row'), 'rhs'), parts along dimension 1
- anc_solution: float32 [768, 2048], P('row', 'rhs'), parts along dimension 1
There are 2 independent parts, one for each index of `rhs`. A program takes and returns all parts, laid end to end along the dimension named above; an argument that names none is the same for every part. Nothing has to cross between parts.
Inputs may be any that keep to these rules, and one draw needn't show every extreme that they name: `block_sizes`: every value lies between 384 and 768; some block row uses all 768 rows and another exactly 384. `anc_rows`: within each block row's 512 entries the ancestor rows are distinct and increasing. `leaf_inverse`: each 768 x 768 block is lower triangular with a unit diagonal. `anc_inverse`: lower triangular with a unit diagonal.
All inputs are finite; a program needn't handle non-finite values.
Results may differ from a plain program's by a relative error of at most 0.0001.
Values sent between devices are 32-bit elements; how exact they have to be, the bound alone decides.
A program may use at most 128 MiB of HBM per device.

v0:
```python
import jax
import jax.numpy as jnp
from jax import lax
from jax.sharding import PartitionSpec as P


def passed_along(array, axis, by):
    devices = lax.axis_size(axis)
    pairs = [(i, i + by) for i in range(devices) if 0 <= i + by < devices]
    return lax.ppermute(array, axis, pairs)


def body(leaf_rhs, block_sizes, leaf_lower, leaf_inverse, coupling, anc_rows, anc_rhs, anc_inverse):
    highest = lax.Precision.HIGHEST
    block_rows = leaf_rhs.shape[0]
    columns = leaf_rhs.shape[1]
    lead_rows = leaf_lower.shape[1]
    anc_count = anc_inverse.shape[0]
    row_devices = lax.axis_size("row")
    position = lax.axis_index("row")
    live_rows = (jnp.arange(block_rows, dtype=jnp.int32) < block_sizes[0]).astype(jnp.float32)
    lower_lead = leaf_lower[:lead_rows]
    inverse_lead = leaf_inverse[:lead_rows, :lead_rows]
    live_lead = live_rows[:lead_rows]
    right_lead = leaf_rhs[:lead_rows]

    def solve_lead(right_cols, carried):
        reduced = right_cols - jnp.dot(
            lower_lead, carried, precision=highest, preferred_element_type=jnp.float32
        )
        solved = jnp.dot(
            inverse_lead, reduced, precision=highest, preferred_element_type=jnp.float32
        )
        return solved * live_lead[:, None]

    block_count = 4
    block_width = columns // block_count

    def advance(iteration, carry):
        carried_all, carried = carry
        column_block = iteration - position
        active = jnp.logical_and(column_block >= 0, column_block < block_count)
        first_col = jnp.clip(column_block, 0, block_count - 1) * block_width
        carried_all = jnp.where(
            active, lax.dynamic_update_slice_in_dim(carried_all, carried, first_col, 1), carried_all
        )
        right_cols = lax.dynamic_slice_in_dim(right_lead, first_col, block_width, 1)
        solved = solve_lead(right_cols, carried)
        carried = passed_along(solved, "row", 1)
        return (carried_all, carried)

    start_carry = (
        jnp.zeros((lead_rows, columns), jnp.float32),
        jnp.zeros((lead_rows, block_width), jnp.float32),
    )
    carried_all, carried = lax.fori_loop(0, row_devices + block_count - 1, advance, start_carry)
    reduced = leaf_rhs - jnp.dot(
        leaf_lower, carried_all, precision=highest, preferred_element_type=jnp.float32
    )
    solved = jnp.dot(leaf_inverse, reduced, precision=highest, preferred_element_type=jnp.float32)
    leaf_solution = solved * live_rows[:, None]
    coupled = jnp.dot(
        coupling, leaf_solution, precision=highest, preferred_element_type=jnp.float32
    )
    one_hot = (jnp.arange(anc_count, dtype=jnp.int32)[:, None] == anc_rows[None, :]).astype(
        jnp.float32
    )
    partial_value = jnp.dot(one_hot, coupled, precision=highest, preferred_element_type=jnp.float32)
    share_rows = anc_count // row_devices
    inverse_rows = lax.dynamic_slice_in_dim(anc_inverse, position * share_rows, share_rows, 0)
    total = lax.psum(partial_value, ("grid", "row"))
    anc_solution = jnp.dot(
        inverse_rows, anc_rhs - total, precision=highest, preferred_element_type=jnp.float32
    )
    return (leaf_solution, anc_solution)


def solution(mesh):
    placed = (
        P(("grid", "row"), "rhs"),
        P(("grid", "row")),
        P(("grid", "row"), None),
        P(("grid", "row"), None),
        P(("grid", "row"), None),
        P(("grid", "row")),
        P(None, "rhs"),
        P(),
    )
    return jax.shard_map(
        body,
        mesh=mesh,
        in_specs=placed,
        out_specs=(P(("grid", "row"), "rhs"), P("row", "rhs")),
        check_vma=False,
    )
```

profile of v0, /device:TPU:0, one launch (start us, length us, event | category | flops | bytes accessed | tf_op | source)
XLA Modules:
  0.0 287.8 jit_solution(9463676214455668131)
XLA Ops:
  7.2 0.0 copy-start
  7.2 0.0 slice-start
  7.2 0.0 all-reduce.2.cloned.1.call-start
  8.1 1.0 slice.14
  9.0 2.3 slice.12
  11.4 1.0 broadcast_in_dim.12
  12.4 0.0 slice-done
  12.4 82.0 %while.15 = (s32[]{:T(128)}, f32[256,1024]{0,1:T(8,128)}, f32[256,256]{0,1:T(8,128)S(1)}, s32[]{:T(128)}, f32[256,1024]{1,0:T(8,128)}, /*index=5*/f32[256,256]{1...) while((s32[]{:T(128)}, f32[256,1024]{0,1:T(8,128)}, ...), condition=%wide.region_1.2_spmd, body=%wide.region_0.1_spmd.sunk | while | flops 402849792 | bytes 4195613 | solution.py:56
  12.4 1.4 convolution_subtract_fusion.2
  13.8 0.6 fusion.31
  14.4 5.6 %collective-permute-start = (f32[256,256]{0,1:T(8,128)S(1)}, f32[256,256]{0,1:T(8,128)}, u32[]{:S(2)}, u32[]{:S(2)}) collective-permute-start(f32[256,256]{0,1:T(8,128)S(1)} %fusion.31), channel_id=1, source_target_pairs={{0,2},{2,4},{4,6},{1,3},{3,5},{5,7},{8,10},{10,12},{12,14},{9,11},... | collective-permute-start | bytes 786440 | tf_op jit(solution)/shard_map/while/body/eval_jaxpr/ppermute | solution.py:10
  20.0 1.7 select_dynamic-update-slice_fusion.2
  21.7 3.2 %collective-permute-done = f32[256,256]{0,1:T(8,128)} collective-permute-done((f32[256,256]{0,1:T(8,128)S(1)}, f32[256,256]{0,1:T(8,128)}, u32[]{:S(2)}, u32[]{:S(2)}) %collective-permute-start) | collective-permute-done | bytes 262176 | tf_op jit(solution)/shard_map/while/body/eval_jaxpr/ppermute | solution.py:10
  24.9 0.9 copy.20
  25.8 1.4 convolution_subtract_fusion.2
  27.2 0.6 fusion.31
  27.8 5.2 %collective-permute-start = (f32[256,256]{0,1:T(8,128)S(1)}, f32[256,256]{0,1:T(8,128)}, u32[]{:S(2)}, u32[]{:S(2)}) collective-permute-start(f32[256,256]{0,1:T(8,128)S(1)} %fusion.31), channel_id=1, source_target_pairs={{0,2},{2,4},{4,6},{1,3},{3,5},{5,7},{8,10},{10,12},{12,14},{9,11},... | collective-permute-start | bytes 786440 | tf_op jit(solution)/shard_map/while/body/eval_jaxpr/ppermute | solution.py:10
  33.0 1.7 select_dynamic-update-slice_fusion.2
  34.7 2.3 collective-permute-done
  37.0 0.9 copy.20
  37.9 1.4 convolution_subtract_fusion.2
  39.3 0.6 fusion.31
  39.9 5.2 %collective-permute-start = (f32[256,256]{0,1:T(8,128)S(1)}, f32[256,256]{0,1:T(8,128)}, u32[]{:S(2)}, u32[]{:S(2)}) collective-permute-start(f32[256,256]{0,1:T(8,128)S(1)} %fusion.31), channel_id=1, source_target_pairs={{0,2},{2,4},{4,6},{1,3},{3,5},{5,7},{8,10},{10,12},{12,14},{9,11},... | collective-permute-start | bytes 786440 | tf_op jit(solution)/shard_map/while/body/eval_jaxpr/ppermute | solution.py:10
  45.1 1.7 select_dynamic-update-slice_fusion.2
  46.8 1.5 collective-permute-done
  48.3 0.9 copy.20
  49.2 1.4 convolution_subtract_fusion.2
  50.6 0.6 fusion.31
  51.2 5.2 %collective-permute-start = (f32[256,256]{0,1:T(8,128)S(1)}, f32[256,256]{0,1:T(8,128)}, u32[]{:S(2)}, u32[]{:S(2)}) collective-permute-start(f32[256,256]{0,1:T(8,128)S(1)} %fusion.31), channel_id=1, source_target_pairs={{0,2},{2,4},{4,6},{1,3},{3,5},{5,7},{8,10},{10,12},{12,14},{9,11},... | collective-permute-start | bytes 786440 | tf_op jit(solution)/shard_map/while/body/eval_jaxpr/ppermute | solution.py:10
  56.4 1.7 select_dynamic-update-slice_fusion.2
  58.1 1.5 collective-permute-done
  59.6 0.9 copy.20
  60.5 1.4 convolution_subtract_fusion.2
  61.9 0.6 fusion.31
  62.5 5.2 %collective-permute-start = (f32[256,256]{0,1:T(8,128)S(1)}, f32[256,256]{0,1:T(8,128)}, u32[]{:S(2)}, u32[]{:S(2)}) collective-permute-start(f32[256,256]{0,1:T(8,128)S(1)} %fusion.31), channel_id=1, source_target_pairs={{0,2},{2,4},{4,6},{1,3},{3,5},{5,7},{8,10},{10,12},{12,14},{9,11},... | collective-permute-start | bytes 786440 | tf_op jit(solution)/shard_map/while/body/eval_jaxpr/ppermute | solution.py:10
  67.7 1.7 select_dynamic-update-slice_fusion.2
  69.4 1.5 collective-permute-done
  70.9 0.9 copy.20
  71.8 1.4 convolution_subtract_fusion.2
  73.2 0.6 fusion.31
  73.8 5.2 %collective-permute-start = (f32[256,256]{0,1:T(8,128)S(1)}, f32[256,256]{0,1:T(8,128)}, u32[]{:S(2)}, u32[]{:S(2)}) collective-permute-start(f32[256,256]{0,1:T(8,128)S(1)} %fusion.31), channel_id=1, source_target_pairs={{0,2},{2,4},{4,6},{1,3},{3,5},{5,7},{8,10},{10,12},{12,14},{9,11},... | collective-permute-start | bytes 786440 | tf_op jit(solution)/shard_map/while/body/eval_jaxpr/ppermute | solution.py:10
  79.0 1.7 select_dynamic-update-slice_fusion.2
  80.7 1.5 collective-permute-done
  82.2 0.9 copy.20
  83.1 1.4 convolution_subtract_fusion.2
  84.5 0.6 fusion.31
  85.1 5.2 %collective-permute-start = (f32[256,256]{0,1:T(8,128)S(1)}, f32[256,256]{0,1:T(8,128)}, u32[]{:S(2)}, u32[]{:S(2)}) collective-permute-start(f32[256,256]{0,1:T(8,128)S(1)} %fusion.31), channel_id=1, source_target_pairs={{0,2},{2,4},{4,6},{1,3},{3,5},{5,7},{8,10},{10,12},{12,14},{9,11},... | collective-permute-start | bytes 786440 | tf_op jit(solution)/shard_map/while/body/eval_jaxpr/ppermute | solution.py:10
  90.3 1.7 select_dynamic-update-slice_fusion.2
  92.0 1.5 collective-permute-done
  93.5 0.9 copy.20
  94.4 4.4 %fusion.12 = f32[1024,768]{0,1:T(8,128)S(1)} fusion(f32[256,1024]{0,1:T(8,128)} %get-tuple-element.141, f32[768,256]{1,0:T(8,128)} %param.12), kind=kOutput, calls=%fused_computation.19 | convolution fusion | flops 2415919104 | bytes 4980736 | tf_op jit(solution)/shard_map/dot_general | solution.py:57
  98.8 0.0 copy-done.2
  98.8 0.0 copy-start.3
  98.8 17.0 %fusion.1 = f32[1024,768]{1,0:T(8,128)S(1)} fusion(f32[768,768]{1,0:T(8,128)} %param.13, f32[768,1024]{1,0:T(8,128)S(1)} %copy-done.2, f32[1024,768]{0,1:T(8,128)S(1)} %fusion.12), kind=kOutput, calls=%fused_computation.5 | convolution fusion | flops 7248543744 | bytes 11796480 | tf_op jit(solution)/shard_map/dot_general | solution.py:60
  115.8 0.0 copy-done.3
  115.8 0.0 copy-start.1
  115.8 0.0 copy-start.4
  115.8 5.1 %fusion.4 = f32[1024,512]{1,0:T(8,128)S(1)} fusion(f32[512,768]{1,0:T(8,128)S(1)} %copy-done.3, f32[1024,768]{1,0:T(8,128)S(1)} %fusion.1, f32[768]{0:T(1024)S(1)} %fusion.10), kind=kOutput, calls=%fused_computation.8 | convolution fusion | flops 4832624640 | bytes 6818816 | tf_op jit(solution)/shard_map/dot_general | solution.py:62
  121.0 4.7 %fusion.7 = f32[768,1024]{1,0:T(8,128)} fusion(f32[1024,512]{1,0:T(8,128)S(1)} %fusion.4, s32[512]{0:T(512)S(1)} %copy-done.4), kind=kOutput, calls=%fused_computation.13 | convolution fusion | flops 4832231424 | bytes 5244928 | tf_op jit(solution)/shard_map/dot_general | solution.py:68
  125.7 0.0 all-reduce.2.cloned.1.call-update
  125.7 3.8 %multiply_bitcast_fusion = f32[768,1024]{0,1:T(8,128)} fusion(f32[1024,768]{1,0:T(8,128)} %copy-done.1, f32[768]{0:T(1024)S(1)} %fusion.10), kind=kLoop, calls=%fused_computation.10 | loop fusion | flops 786432 | bytes 6294528 | tf_op jit(solution)/shard_map/mul | solution.py:61
  129.5 3.5 %copy.10 = f32[768,1024]{1,0:T(8,128)} copy(f32[768,1024]{0,1:T(8,128)} %multiply_bitcast_fusion) | data formatting | bytes 6291456
  133.0 142.0 %all-reduce.2.cloned.1.call-done = f32[768,1024]{1,0:T(8,128)} async-done(((f32[768,1024]{1,0:T(8,128)}), f32[768,1024]{1,0:T(8,128)}) %all-reduce.2.cloned.1.call-update) | async-done | bytes 3145744 | tf_op jit(solution)/shard_map/psum | solution.py:71
  275.0 6.0 %fusion.2 = f32[192,1024]{1,0:T(8,128)} fusion(f32[768,1024]{1,0:T(8,128)} %param.16, f32[768,1024]{1,0:T(8,128)} %all-reduce.2.cloned.1.call-done, f32[768,768]{1,0:T(8,128)S(1)} %copy-done, s32[]{:T(128)S(6)} %select_n.27), kind=kOutput, calls=%fused_computation.6 | convolution fusion | flops 1812725760 | bytes 7667716 | tf_op jit(solution)/shard_map/dot_general | solution.py:72
  (7 shorter events, 0.0 us)
Async XLA Ops:
  7.2 267.8 %copy-start = (f32[768,768]{1,0:T(8,128)S(1)}, f32[768,768]{1,0:T(8,128)}, u32[]{:S(2)}) copy-start(f32[768,768]{1,0:T(8,128)} %param.17) | copy-start | bytes 7077892
  7.2 5.2 %slice-start = ((f32[768,256]{1,0:T(8,128)}), f32[256,256]{1,0:T(8,128)S(1)}, s32[]{:S(2)}) async-start(f32[768,256]{1,0:T(8,128)} %param.12), calls=%async_computation.1 | async-start | bytes 524288 | tf_op jit(solution)/shard_map/slice | solution.py:22
  7.2 267.8 %all-reduce.2.cloned.1.call-start = ((), (), s32[]{:S(2)}) async-start(), calls=%async_computation | async-start | bytes 6291456 | tf_op jit(solution)/shard_map/psum | solution.py:71
  14.4 10.5 %collective-permute-start = (f32[256,256]{0,1:T(8,128)S(1)}, f32[256,256]{0,1:T(8,128)}, u32[]{:S(2)}, u32[]{:S(2)}) collective-permute-start(f32[256,256]{0,1:T(8,128)S(1)} %fusion.31), channel_id=1, source_target_pairs={{0,2},{2,4},{4,6},{1,3},{3,5},{5,7},{8,10},{10,12},{12,14},{9,11},... | collective-permute-start | bytes 786440 | tf_op jit(solution)/shard_map/while/body/eval_jaxpr/ppermute | solution.py:10
  27.8 9.2 %collective-permute-start = (f32[256,256]{0,1:T(8,128)S(1)}, f32[256,256]{0,1:T(8,128)}, u32[]{:S(2)}, u32[]{:S(2)}) collective-permute-start(f32[256,256]{0,1:T(8,128)S(1)} %fusion.31), channel_id=1, source_target_pairs={{0,2},{2,4},{4,6},{1,3},{3,5},{5,7},{8,10},{10,12},{12,14},{9,11},... | collective-permute-start | bytes 786440 | tf_op jit(solution)/shard_map/while/body/eval_jaxpr/ppermute | solution.py:10
  39.9 8.4 %collective-permute-start = (f32[256,256]{0,1:T(8,128)S(1)}, f32[256,256]{0,1:T(8,128)}, u32[]{:S(2)}, u32[]{:S(2)}) collective-permute-start(f32[256,256]{0,1:T(8,128)S(1)} %fusion.31), channel_id=1, source_target_pairs={{0,2},{2,4},{4,6},{1,3},{3,5},{5,7},{8,10},{10,12},{12,14},{9,11},... | collective-permute-start | bytes 786440 | tf_op jit(solution)/shard_map/while/body/eval_jaxpr/ppermute | solution.py:10
  51.2 8.4 %collective-permute-start = (f32[256,256]{0,1:T(8,128)S(1)}, f32[256,256]{0,1:T(8,128)}, u32[]{:S(2)}, u32[]{:S(2)}) collective-permute-start(f32[256,256]{0,1:T(8,128)S(1)} %fusion.31), channel_id=1, source_target_pairs={{0,2},{2,4},{4,6},{1,3},{3,5},{5,7},{8,10},{10,12},{12,14},{9,11},... | collective-permute-start | bytes 786440 | tf_op jit(solution)/shard_map/while/body/eval_jaxpr/ppermute | solution.py:10
  62.5 8.4 %collective-permute-start = (f32[256,256]{0,1:T(8,128)S(1)}, f32[256,256]{0,1:T(8,128)}, u32[]{:S(2)}, u32[]{:S(2)}) collective-permute-start(f32[256,256]{0,1:T(8,128)S(1)} %fusion.31), channel_id=1, source_target_pairs={{0,2},{2,4},{4,6},{1,3},{3,5},{5,7},{8,10},{10,12},{12,14},{9,11},... | collective-permute-start | bytes 786440 | tf_op jit(solution)/shard_map/while/body/eval_jaxpr/ppermute | solution.py:10
  73.8 8.4 %collective-permute-start = (f32[256,256]{0,1:T(8,128)S(1)}, f32[256,256]{0,1:T(8,128)}, u32[]{:S(2)}, u32[]{:S(2)}) collective-permute-start(f32[256,256]{0,1:T(8,128)S(1)} %fusion.31), channel_id=1, source_target_pairs={{0,2},{2,4},{4,6},{1,3},{3,5},{5,7},{8,10},{10,12},{12,14},{9,11},... | collective-permute-start | bytes 786440 | tf_op jit(solution)/shard_map/while/body/eval_jaxpr/ppermute | solution.py:10
  85.1 8.4 %collective-permute-start = (f32[256,256]{0,1:T(8,128)S(1)}, f32[256,256]{0,1:T(8,128)}, u32[]{:S(2)}, u32[]{:S(2)}) collective-permute-start(f32[256,256]{0,1:T(8,128)S(1)} %fusion.31), channel_id=1, source_target_pairs={{0,2},{2,4},{4,6},{1,3},{3,5},{5,7},{8,10},{10,12},{12,14},{9,11},... | collective-permute-start | bytes 786440 | tf_op jit(solution)/shard_map/while/body/eval_jaxpr/ppermute | solution.py:10
  94.4 4.4 %copy-start.2 = (f32[768,1024]{1,0:T(8,128)S(1)}, f32[768,1024]{1,0:T(8,128)}, u32[]{:S(2)}) copy-start(f32[768,1024]{1,0:T(8,128)} %param.10) | copy-start | bytes 9437188
  98.8 17.0 %copy-start.3 = (f32[512,768]{1,0:T(8,128)S(1)}, f32[512,768]{1,0:T(8,128)}, u32[]{:S(2)}) copy-start(f32[512,768]{1,0:T(8,128)} %param.14) | copy-start | bytes 4718596
  115.8 5.1 %copy-start.1 = (f32[1024,768]{1,0:T(8,128)}, f32[1024,768]{1,0:T(8,128)S(1)}, u32[]{:S(2)}) copy-start(f32[1024,768]{1,0:T(8,128)S(1)} %fusion.1) | copy-start | bytes 9437188
  115.8 5.1 %copy-start.4 = (s32[512]{0:T(512)S(1)}, s32[512]{0:T(512)}, u32[]{:S(2)}) copy-start(s32[512]{0:T(512)} %param.15) | copy-start | bytes 6148
Sparse Core Ops, SparseCore 0:
  125.8 149.1 all-reduce.1
where the time goes:
time: 289 us; the launch traced here: 288 us
  waiting for transfers between devices  155 us (54%)
  matrix products  50.9 us (18%)
  starting transfers between devices  36.9 us (13%)
  other arithmetic  15.6 us (5%)
  between operations  14.9 us (5%)
  local copies, waits for them, and re-layouts  14.6 us (5%)
    psum x1, waiting for transfers between devices, body(): total = lax.psum(partial_value, ('grid', 'row'))  142 us
    ppermute x7, starting transfers between devices, passed_along(): return lax.ppermute(array, axis, pairs)  36.9 us
    dot_general x1, matrix products, body(): jnp.dot(leaf_inverse, reduced, precision=highest, preferred_element_type=...  17 us
    ppermute x7, waiting for transfers between devices, passed_along(): return lax.ppermute(array, axis, pairs)  12.8 us
    select_n x7, other arithmetic, advance(): jnp.where(active, lax.dynamic_update_slice_in_dim(carried_all, carried, f...  11.8 us
    dot_general x7, matrix products, solve_lead(): jnp.dot(lower_lead, carried, precision=highest, preferred_element_type=jn...  9.52 us
    while x7, local copies, waits for them, and re-layouts  6.65 us
    dot_general x1, matrix products, body(): jnp.dot(inverse_rows, anc_rhs - total, precision=highest, preferred_eleme...  6 us
  transfers between devices with their start and end apart: 8, of which 8 were waited for; matrix products, arithmetic and copies ran while one was open for 7% of the time, Pallas kernels for 0%

commit v1 on v0

v1 whole, which is shorter than its diff:
```python
import functools

import jax
import jax.numpy as jnp
from jax import lax
from jax.experimental import pallas as pl
from jax.experimental.pallas import tpu as pltpu
from jax.sharding import PartitionSpec as P

MESH = pl.DeviceIdType.MESH
F32 = jnp.float32
BF16 = jnp.bfloat16
CHUNK = 128
TILE = 256


def split(value):
    high = value.astype(BF16)
    return high, (value - high.astype(F32)).astype(BF16)


def dot(left, right):
    return jnp.dot(left, right, preferred_element_type=F32)


def dot_split(left_high, left_low, right_high, right_low):
    small = dot(left_high, right_low) + dot(left_low, right_high)
    return dot(left_high, right_high) + small


def triangle(high_ref, low_ref, tile, right_high, right_low):
    rows = pl.ds(tile * TILE, TILE)
    depth = (tile + 1) * TILE
    return dot_split(
        high_ref[rows, :depth], low_ref[rows, :depth], right_high[:depth], right_low[:depth]
    )


def kernel(
    n_grid, n_row,
    size_ref, rows_ref, rhs_hbm, lower_hbm, inverse_hbm, coupling_hbm, anc_rhs_hbm, anc_inverse_hbm,
    leaf_hbm, anc_ref,
    rhs, lower, inverse, coupling, anc_rhs, anc_inverse,
    inv_high, inv_low, step_high, step_low, onto_high, onto_low, anc_high, anc_low,
    leaf, carried, stage, summed, shares, shares_in, final, final_in,
    load_sem, anc_sem, leaf_sem, chain_send, chain_recv, sum_send, sum_recv,
    share_send, share_recv, final_send, final_recv,
):
    grid, row = lax.axis_index("grid"), lax.axis_index("row")
    block_rows, columns = leaf.shape
    lead = carried.shape[0]
    count = columns // CHUNK
    pairs = count // 2
    owned = count // n_grid
    cycle = n_grid // 2
    share = anc_ref.shape[0]
    tiles = block_rows // TILE
    anc_tiles = anc_high.shape[0] // TILE
    wide = 2 * CHUNK

    def chunk_cols(chunk):
        return pl.ds(pl.multiple_of(chunk * CHUNK, CHUNK), CHUNK)

    def pair_cols(pair):
        return pl.ds(pl.multiple_of(pair * wide, wide), wide)

    def pair_of(turn):
        return (turn // cycle) * cycle + lax.rem(lax.rem(turn, cycle) + grid // 2 + 1, cycle)

    loads = [
        pltpu.make_async_copy(inverse_hbm, inverse, load_sem.at[0]),
        pltpu.make_async_copy(rhs_hbm.at[:lead], rhs.at[:lead], load_sem.at[1]),
        pltpu.make_async_copy(lower_hbm, lower, load_sem.at[2]),
        pltpu.make_async_copy(rhs_hbm.at[lead:], rhs.at[lead:], load_sem.at[3]),
        pltpu.make_async_copy(coupling_hbm, coupling, load_sem.at[4]),
        pltpu.make_async_copy(anc_inverse_hbm, anc_inverse, load_sem.at[5]),
    ]
    for load in loads:
        load.start()
    anc_loads = [
        pltpu.make_async_copy(
            anc_rhs_hbm.at[:, chunk_cols(u * n_grid + grid)], anc_rhs.at[u], anc_sem.at[u]
        )
        for u in range(owned)
    ]
    for load in anc_loads:
        load.start()

    barrier = pltpu.get_barrier_semaphore()
    for off in range(1, n_grid):
        pl.semaphore_signal(
            barrier, inc=1, device_id={"grid": lax.rem(grid + off, n_grid)}, device_id_type=MESH
        )
    for off in range(1, n_row):
        pl.semaphore_signal(
            barrier, inc=1, device_id={"row": lax.rem(row + off, n_row)}, device_id_type=MESH
        )
    pl.semaphore_wait(barrier, n_grid + n_row - 2)

    def chain_copy(chunk):
        return pltpu.make_async_remote_copy(
            src_ref=leaf.at[pl.ds(0, lead), chunk_cols(chunk)],
            dst_ref=carried.at[:, chunk_cols(chunk)],
            send_sem=chain_send.at[chunk],
            recv_sem=chain_recv.at[chunk],
            device_id={"row": lax.rem(row + 1, n_row)},
            device_id_type=MESH,
        )

    def sum_copy(chunk):
        owner = lax.rem(chunk, n_grid)
        off = lax.rem(owner - grid + n_grid, n_grid)
        part = chunk // n_grid
        return off, pltpu.make_async_remote_copy(
            src_ref=stage.at[chunk],
            dst_ref=summed.at[part, off],
            send_sem=sum_send.at[chunk],
            recv_sem=sum_recv.at[part, off],
            device_id={"grid": owner},
            device_id_type=MESH,
        )

    def share_copy(part, off):
        target = lax.rem(row + off, n_row)
        return pltpu.make_async_remote_copy(
            src_ref=shares.at[part, target],
            dst_ref=shares_in.at[part, off],
            send_sem=share_send.at[part, off],
            recv_sem=share_recv.at[part, off],
            device_id={"row": target},
            device_id_type=MESH,
        )

    def final_copy(part, off):
        return pltpu.make_async_remote_copy(
            src_ref=final.at[part],
            dst_ref=final_in.at[part, off],
            send_sem=final_send.at[part, off],
            recv_sem=final_recv.at[part, off],
            device_id={"grid": lax.rem(grid + off, n_grid)},
            device_id_type=MESH,
        )

    def leaf_copy(pair):
        return pltpu.make_async_copy(
            leaf.at[:, pair_cols(pair)], leaf_hbm.at[:, pair_cols(pair)], leaf_sem.at[pair]
        )

    size = size_ref[0]

    def prepare(tile):
        rows = pl.ds(tile * TILE, TILE)
        depth = (tile + 1) * TILE
        place = lax.broadcasted_iota(jnp.int32, (TILE, depth), 0) + tile * TILE
        live = jnp.where(place < size, inverse[rows, :depth], 0.0)
        inv_high[rows, :depth], inv_low[rows, :depth] = split(live)

    loads[0].wait()
    prepare(0)
    loads[1].wait()

    @pl.loop(0, pairs)
    def _(turn):
        pair = pair_of(turn)
        cols = pair_cols(pair)
        high, low = split(rhs[pl.ds(0, TILE), cols])
        leaf[pl.ds(0, TILE), cols] = triangle(inv_high, inv_low, 0, high, low)

        @pl.when(row == 0)
        def _():
            chain_copy(2 * pair).start()
            chain_copy(2 * pair + 1).start()

    for tile in range(1, tiles):
        prepare(tile)
    loads[2].wait()
    lower_high, lower_low = split(lower[...])
    for tile in range(tiles):
        rows = pl.ds(tile * TILE, TILE)
        step = triangle(inv_high, inv_low, tile, lower_high, lower_low)
        step_high[rows, :], step_low[rows, :] = split(step)
    loads[3].wait()

    @pl.loop(0, pairs)
    def _(turn):
        cols = pair_cols(pair_of(turn))
        high, low = split(rhs[:, cols])
        for tile in range(1, tiles):
            leaf[pl.ds(tile * TILE, TILE), cols] = triangle(inv_high, inv_low, tile, high, low)

    loads[4].wait()
    coupling_high, coupling_low = split(coupling[...])
    for tile in range(anc_tiles):
        rows = pl.ds(tile * TILE, TILE)
        place = lax.broadcasted_iota(jnp.int32, (TILE, coupling.shape[0]), 0) + tile * TILE
        chosen = jnp.where(place == rows_ref[...], 1.0, 0.0).astype(BF16)
        onto_high[rows, :] = dot(chosen, coupling_high).astype(BF16)
        onto_low[rows, :] = dot(chosen, coupling_low).astype(BF16)
    loads[5].wait()
    anc_high[...], anc_low[...] = split(anc_inverse[...])

    @pl.loop(0, pairs)
    def _(turn):
        pair = pair_of(turn)
        cols = pair_cols(pair)

        @pl.when(row > 0)
        def _():
            for side in range(2):
                chunk = 2 * pair + side
                chain_copy(chunk).wait_recv()
                high, low = split(carried[:, chunk_cols(chunk)])
                lead_rows = pl.ds(0, TILE)
                leaf[lead_rows, chunk_cols(chunk)] -= dot_split(
                    step_high[lead_rows, :], step_low[lead_rows, :], high, low
                )

                @pl.when(row < n_row - 1)
                def _():
                    chain_copy(chunk).start()

            high, low = split(carried[:, cols])
            for tile in range(1, tiles):
                rows = pl.ds(tile * TILE, TILE)
                leaf[rows, cols] -= dot_split(step_high[rows, :], step_low[rows, :], high, low)

        leaf_copy(pair).start()
        high, low = split(leaf[:, cols])
        for tile in range(anc_tiles):
            rows = pl.ds(tile * TILE, TILE)
            part = dot_split(onto_high[rows, :], onto_low[rows, :], high, low)
            stage[2 * pair, rows, :] = part[:, :CHUNK]
            stage[2 * pair + 1, rows, :] = part[:, CHUNK:]
        for side in range(2):
            off, copy = sum_copy(2 * pair + side)

            @pl.when(off != 0)
            def _():
                copy.start()

    for load in anc_loads:
        load.wait()

    @pl.loop(0, owned)
    def _(part):
        mine = part * n_grid + grid
        for off in range(1, n_grid):
            pltpu.make_async_remote_copy(
                src_ref=stage.at[mine],
                dst_ref=summed.at[part, off],
                send_sem=sum_send.at[mine],
                recv_sem=sum_recv.at[part, off],
                device_id={"grid": lax.rem(grid + off, n_grid)},
                device_id_type=MESH,
            ).wait_recv()
        total = stage[mine] - jnp.where(row == 0, anc_rhs[part], 0.0)
        for off in range(1, n_grid):
            total += summed[part, off]
        high, low = split(total)
        for tile in range(anc_tiles):
            result = triangle(anc_high, anc_low, tile, high, low)
            rows_of(shares, part, tile * TILE, share, result)
        for off in range(1, n_row):
            share_copy(part, off).start()
        own = shares[part, row]
        for off in range(1, n_row):
            share_copy(part, off).wait_recv()
            own += shares_in[part, off]
        final[part] = -own
        for off in range(1, n_grid):
            final_copy(part, off).start()
        anc_ref[:, chunk_cols(mine)] = -own

    @pl.loop(0, owned)
    def _(part):
        for off in range(1, n_grid):
            final_copy(part, off).wait_recv()
            source = part * n_grid + lax.rem(grid - off + n_grid, n_grid)
            anc_ref[:, chunk_cols(source)] = final_in[part, off]
        for off in range(1, n_grid):
            final_copy(part, off).wait_send()
        for off in range(1, n_row):
            share_copy(part, off).wait_send()

    @pl.loop(0, pairs)
    def _(pair):
        leaf_copy(pair).wait()
        for side in range(2):
            chunk = 2 * pair + side

            @pl.when(row < n_row - 1)
            def _():
                chain_copy(chunk).wait_send()

            off, copy = sum_copy(chunk)

            @pl.when(off != 0)
            def _():
                copy.wait_send()


def rows_of(shares, part, first, share, result):
    row, end = first, first + result.shape[0]
    while row < end:
        index, inside = divmod(row, share)
        length = min(share - inside, end - row)
        shares[part, index, inside:inside + length, :] = result[row - first:row - first + length]
        row += length


def body(leaf_rhs, block_sizes, leaf_lower, leaf_inverse, coupling, anc_rows, anc_rhs, anc_inverse):
    n_grid, n_row = lax.axis_size("grid"), lax.axis_size("row")
    block_rows, columns = leaf_rhs.shape
    lead = leaf_lower.shape[1]
    touched = coupling.shape[0]
    anc = anc_inverse.shape[0]
    share = anc // n_row
    count = columns // CHUNK
    owned = count // n_grid
    vmem, dma = pltpu.VMEM, pltpu.SemaphoreType.DMA
    hbm = pl.BlockSpec(memory_space=pl.ANY)
    return pl.pallas_call(
        functools.partial(kernel, n_grid, n_row),
        out_shape=(
            jax.ShapeDtypeStruct((block_rows, columns), F32),
            jax.ShapeDtypeStruct((share, columns), F32),
        ),
        in_specs=[
            pl.BlockSpec(memory_space=pltpu.SMEM),
            pl.BlockSpec(memory_space=pltpu.VMEM),
            hbm, hbm, hbm, hbm, hbm, hbm,
        ],
        out_specs=(hbm, pl.BlockSpec(memory_space=pltpu.VMEM)),
        scratch_shapes=[
            vmem((block_rows, columns), F32),
            vmem((block_rows, lead), F32),
            vmem((block_rows, block_rows), F32),
            vmem((touched, block_rows), F32),
            vmem((owned, anc, CHUNK), F32),
            vmem((anc, anc), F32),
            vmem((block_rows, block_rows), BF16),
            vmem((block_rows, block_rows), BF16),
            vmem((block_rows, lead), BF16),
            vmem((block_rows, lead), BF16),
            vmem((anc, block_rows), BF16),
            vmem((anc, block_rows), BF16),
            vmem((anc, anc), BF16),
            vmem((anc, anc), BF16),
            vmem((block_rows, columns), F32),
            vmem((lead, columns), F32),
            vmem((count, anc, CHUNK), F32),
            vmem((owned, n_grid, anc, CHUNK), F32),
            vmem((owned, n_row, share, CHUNK), F32),
            vmem((owned, n_row, share, CHUNK), F32),
            vmem((owned, share, CHUNK), F32),
            vmem((owned, n_grid, share, CHUNK), F32),
            dma((6,)),
            dma((owned,)),
            dma((count // 2,)),
            dma((count,)),
            dma((count,)),
            dma((count,)),
            dma((owned, n_grid)),
            dma((owned, n_row)),
            dma((owned, n_row)),
            dma((owned, n_grid)),
            dma((owned, n_grid)),
        ],
        compiler_params=pltpu.CompilerParams(
            collective_id=0, has_side_effects=True, vmem_limit_bytes=56 * 1024 * 1024
        ),
        name="forward_solve",
    )(
        block_sizes, anc_rows.reshape(1, touched), leaf_rhs, leaf_lower, leaf_inverse, coupling,
        anc_rhs, anc_inverse,
    )


def solution(mesh):
    placed = (
        P(("grid", "row"), "rhs"),
        P(("grid", "row")),
        P(("grid", "row"), None),
        P(("grid", "row"), None),
        P(("grid", "row"), None),
        P(("grid", "row")),
        P(None, "rhs"),
        P(),
    )
    return jax.shard_map(
        body,
        mesh=mesh,
        in_specs=placed,
        out_specs=(P(("grid", "row"), "rhs"), P("row", "rhs")),
        check_vma=False,
    )
```

time: 289 us -> 82.1 us (0.28)
  waiting for transfers between devices: 155 us -> 0 us
  Pallas kernels: 0 us -> 75.7 us
  matrix products: 50.9 us -> 0 us
  starting transfers between devices: 36.9 us -> 0 us
  other arithmetic: 15.6 us -> 0 us
  between operations: 14.9 us -> 1.29 us
  local copies, waits for them, and re-layouts: 14.6 us -> 4.93 us
    psum x1 -> x0, waiting for transfers between devices: 142 us -> none  [body(): total = lax.psum(partial_value, ('grid', 'row'))]
    pallas_call x0 -> x1, Pallas kernels: none -> 75.7 us  [body(): pl.pallas_call(functools.partial(kernel, n_grid, n_row), out_shape=(jax.S...]
    dot_general x19 -> x0, matrix products: 50.9 us -> none  [the longest x1 17 us: body(): jnp.dot(leaf_inverse, reduced, precision=highest, preferred_element_type=...]
    ppermute x7 -> x0, starting transfers between devices: 36.9 us -> none  [passed_along(): return lax.ppermute(array, axis, pairs)]
    ppermute x7 -> x0, waiting for transfers between devices: 12.8 us -> none  [passed_along(): return lax.ppermute(array, axis, pairs)]
    select_n x7 -> x0, other arithmetic: 11.8 us -> none  [advance(): jnp.where(active, lax.dynamic_update_slice_in_dim(carried_all, carried, f...]
    while x7 -> x0, local copies, waits for them, and re-layouts: 6.65 us -> none
    mul x1 -> x0, other arithmetic: 3.8 us -> none  [body(): leaf_solution = solved * live_rows[:, None]]
  transfers between devices with their start and end apart: 8 -> 0, of which waited for: 8 -> 0; matrix products, arithmetic and copies ran while one was open for 7% -> 0% of each run, Pallas kernels for 0% -> 0%
where the time goes in v1:
time: 82.1 us; the launch traced here: 81.9 us
  Pallas kernels  75.7 us (92%)
  local copies, waits for them, and re-layouts  4.93 us (6%)
  between operations  1.29 us (2%)
    pallas_call x1, Pallas kernels, body(): pl.pallas_call(functools.partial(kernel, n_grid, n_row), out_shape=(jax.S...  75.7 us
    unnamed x4, local copies, waits for them, and re-layouts  4.93 us

profile of v1, /device:TPU:0, one launch (start us, length us, event | category | flops | bytes accessed | tf_op | source)
XLA Modules:
  0.0 81.9 jit_solution(5278736569961039158)
XLA Ops:
  1.3 75.7 %forward_solve.1 = (f32[768,1024]{1,0:T(8,128)}, f32[192,1024]{1,0:T(8,128)}) custom-call(s32[1]{0:T(128)S(6)} %copy.12.size_ref, s32[1,512]{1,0:T(1,128)} %bitcast.1, f32[768,1024]{1,0:T(8,128)} %rhs_hbm.1, f32[768,256]{1,0:T(8,128)} %lower_hbm.1, f32[768,768]{1,0:T(8,128)} %inverse_hbm.1, f32[512,768]{1,0:T(8,128)} %coupling_hbm.1, ...), custom_call_target="tpu_custom_call" | custom-call | tf_op jit(solution)/shard_map/forward_solve/pallas_call | solution.py:322
  77.0 0.0 copy-start
  77.0 4.0 %copy.13 = f32[768,1024]{1,0:T(8,128)} copy(f32[768,1024]{1,0:T(8,128)} %get-tuple-element.4) | data formatting | bytes 6291456
  81.0 0.0 copy-done
  81.0 0.9 %copy.14 = f32[192,1024]{1,0:T(8,128)} copy(f32[192,1024]{1,0:T(8,128)S(1)} %copy-done) | data formatting | bytes 1572864
Async XLA Ops:
  77.0 4.1 %copy-start = (f32[192,1024]{1,0:T(8,128)S(1)}, f32[192,1024]{1,0:T(8,128)}, u32[]{:S(2)}) copy-start(f32[192,1024]{1,0:T(8,128)} %get-tuple-element.5) | copy-start | bytes 2359300

commit v2 on v1

--- a/solution.py
+++ b/solution.py
@@ -41,7 +41,7 @@
     size_ref, rows_ref, rhs_hbm, lower_hbm, inverse_hbm, coupling_hbm, anc_rhs_hbm, anc_inverse_hbm,
     leaf_hbm, anc_ref,
     rhs, lower, inverse, coupling, anc_rhs, anc_inverse,
-    inv_high, inv_low, step_high, step_low, onto_high, onto_low, anc_high, anc_low,
+    coupling_high, coupling_low, inv_high, inv_low, step_high, step_low, onto_high, onto_low, anc_high, anc_low,
     leaf, carried, stage, summed, shares, shares_in, final, final_in,
     load_sem, anc_sem, leaf_sem, chain_send, chain_recv, sum_send, sum_recv,
     share_send, share_recv, final_send, final_recv,
@@ -67,23 +67,26 @@
     def pair_of(turn):
         return (turn // cycle) * cycle + lax.rem(lax.rem(turn, cycle) + grid // 2 + 1, cycle)
 
+    first = [
+        pltpu.make_async_copy(
+            inverse_hbm.at[:TILE, :TILE], inverse.at[:TILE, :TILE], load_sem.at[0]
+        ),
+        pltpu.make_async_copy(rhs_hbm.at[:lead], rhs.at[:lead], load_sem.at[1]),
+    ]
     loads = [
-        pltpu.make_async_copy(inverse_hbm, inverse, load_sem.at[0]),
-        pltpu.make_async_copy(rhs_hbm.at[:lead], rhs.at[:lead], load_sem.at[1]),
         pltpu.make_async_copy(lower_hbm, lower, load_sem.at[2]),
-        pltpu.make_async_copy(rhs_hbm.at[lead:], rhs.at[lead:], load_sem.at[3]),
-        pltpu.make_async_copy(coupling_hbm, coupling, load_sem.at[4]),
-        pltpu.make_async_copy(anc_inverse_hbm, anc_inverse, load_sem.at[5]),
+        pltpu.make_async_copy(inverse_hbm.at[TILE:], inverse.at[TILE:], load_sem.at[3]),
+        pltpu.make_async_copy(rhs_hbm.at[lead:], rhs.at[lead:], load_sem.at[4]),
+        pltpu.make_async_copy(coupling_hbm, coupling, load_sem.at[5]),
+        pltpu.make_async_copy(anc_inverse_hbm, anc_inverse, load_sem.at[6]),
     ]
-    for load in loads:
-        load.start()
     anc_loads = [
         pltpu.make_async_copy(
             anc_rhs_hbm.at[:, chunk_cols(u * n_grid + grid)], anc_rhs.at[u], anc_sem.at[u]
         )
         for u in range(owned)
     ]
-    for load in anc_loads:
+    for load in first:
         load.start()
 
     barrier = pltpu.get_barrier_semaphore()
@@ -155,9 +158,11 @@
         live = jnp.where(place < size, inverse[rows, :depth], 0.0)
         inv_high[rows, :depth], inv_low[rows, :depth] = split(live)
 
-    loads[0].wait()
+    for load in first:
+        load.wait()
+    for load in loads + anc_loads:
+        load.start()
     prepare(0)
-    loads[1].wait()
 
     @pl.loop(0, pairs)
     def _(turn):
@@ -171,54 +176,51 @@
             chain_copy(2 * pair).start()
             chain_copy(2 * pair + 1).start()
 
-    for tile in range(1, tiles):
-        prepare(tile)
-    loads[2].wait()
+    loads[0].wait()
     lower_high, lower_low = split(lower[...])
+    loads[1].wait()
     for tile in range(tiles):
+        if tile > 0:
+            prepare(tile)
         rows = pl.ds(tile * TILE, TILE)
         step = triangle(inv_high, inv_low, tile, lower_high, lower_low)
         step_high[rows, :], step_low[rows, :] = split(step)
-    loads[3].wait()
-
-    @pl.loop(0, pairs)
-    def _(turn):
+    for load in loads[2:]:
+        load.wait()
+    coupling_high[...], coupling_low[...] = split(coupling[...])
+
+    def follow(index):
+        chunk = 2 * pair_of(index // 2) + lax.rem(index, 2)
+        chain_copy(chunk).wait_recv()
+        high, low = split(carried[:, chunk_cols(chunk)])
+        lead_rows = pl.ds(0, TILE)
+        leaf[lead_rows, chunk_cols(chunk)] -= dot_split(
+            step_high[lead_rows, :], step_low[lead_rows, :], high, low
+        )
+
+        @pl.when(row < n_row - 1)
+        def _():
+            chain_copy(chunk).start()
+
+    def rest(turn):
         cols = pair_cols(pair_of(turn))
         high, low = split(rhs[:, cols])
         for tile in range(1, tiles):
             leaf[pl.ds(tile * TILE, TILE), cols] = triangle(inv_high, inv_low, tile, high, low)
 
-    loads[4].wait()
-    coupling_high, coupling_low = split(coupling[...])
-    for tile in range(anc_tiles):
-        rows = pl.ds(tile * TILE, TILE)
+    def spread(tile):
+        rows = pl.ds(pl.multiple_of(tile * TILE, TILE), TILE)
         place = lax.broadcasted_iota(jnp.int32, (TILE, coupling.shape[0]), 0) + tile * TILE
         chosen = jnp.where(place == rows_ref[...], 1.0, 0.0).astype(BF16)
-        onto_high[rows, :] = dot(chosen, coupling_high).astype(BF16)
-        onto_low[rows, :] = dot(chosen, coupling_low).astype(BF16)
-    loads[5].wait()
-    anc_high[...], anc_low[...] = split(anc_inverse[...])
-
-    @pl.loop(0, pairs)
-    def _(turn):
+        onto_high[rows, :] = dot(chosen, coupling_high[...]).astype(BF16)
+        onto_low[rows, :] = dot(chosen, coupling_low[...]).astype(BF16)
+
+    def couple(turn):
         pair = pair_of(turn)
         cols = pair_cols(pair)
 
         @pl.when(row > 0)
         def _():
-            for side in range(2):
-                chunk = 2 * pair + side
-                chain_copy(chunk).wait_recv()
-                high, low = split(carried[:, chunk_cols(chunk)])
-                lead_rows = pl.ds(0, TILE)
-                leaf[lead_rows, chunk_cols(chunk)] -= dot_split(
-                    step_high[lead_rows, :], step_low[lead_rows, :], high, low
-                )
-
-                @pl.when(row < n_row - 1)
-                def _():
-                    chain_copy(chunk).start()
-
             high, low = split(carried[:, cols])
             for tile in range(1, tiles):
                 rows = pl.ds(tile * TILE, TILE)
@@ -237,6 +239,40 @@
             @pl.when(off != 0)
             def _():
                 copy.start()
+
+    @pl.loop(0, count + n_row - 2)
+    def _(beat):
+        index = beat + 1 - row
+
+        @pl.when(jnp.logical_and(row > 0, jnp.logical_and(index >= 0, index < count)))
+        def _():
+            follow(index)
+
+        @pl.when(beat < anc_tiles)
+        def _():
+            spread(beat)
+
+        @pl.when(beat < pairs)
+        def _():
+            rest(beat)
+
+        @pl.when(beat == anc_tiles)
+        def _():
+            anc_high[...], anc_low[...] = split(anc_inverse[...])
+
+        early = beat - pairs
+        is_early = jnp.logical_and(
+            jnp.logical_and(early >= 0, early < pairs), early + row <= pairs
+        )
+        late = (beat + n_row - row) // 2 - n_row // 2
+        is_late = jnp.logical_and(
+            jnp.logical_and(late >= 0, late < pairs),
+            jnp.logical_and(late * 2 + row == beat, late + row > pairs),
+        )
+
+        @pl.when(jnp.logical_or(is_early, is_late))
+        def _():
+            couple(jnp.where(is_early, early, late))
 
     for load in anc_loads:
         load.wait()
@@ -338,6 +374,8 @@
             vmem((touched, block_rows), F32),
             vmem((owned, anc, CHUNK), F32),
             vmem((anc, anc), F32),
+            vmem((touched, block_rows), BF16),
+            vmem((touched, block_rows), BF16),
             vmem((block_rows, block_rows), BF16),
             vmem((block_rows, block_rows), BF16),
             vmem((block_rows, lead), BF16),
@@ -354,7 +392,7 @@
             vmem((owned, n_row, share, CHUNK), F32),
             vmem((owned, share, CHUNK), F32),
             vmem((owned, n_grid, share, CHUNK), F32),
-            dma((6,)),
+            dma((7,)),
             dma((owned,)),
             dma((count // 2,)),
             dma((count,)),

time: 82.1 us -> 85 us (1.035)
  Pallas kernels: 75.7 us -> 78.6 us
    pallas_call x1, Pallas kernels: 75.7 us -> 78.6 us  [body(): pl.pallas_call(functools.partial(kernel, n_grid, n_row), out_shape=(jax.S...]
where the time goes in v2:
time: 85 us; the launch traced here: 84.9 us
  Pallas kernels  78.6 us (92%)
  local copies, waits for them, and re-layouts  4.93 us (6%)
  between operations  1.29 us (2%)
    pallas_call x1, Pallas kernels, body(): pl.pallas_call(functools.partial(kernel, n_grid, n_row), out_shape=(jax.S...  78.6 us
    unnamed x4, local copies, waits for them, and re-layouts  4.93 us

profile of v2, /device:TPU:0, one launch (start us, length us, event | category | flops | bytes accessed | tf_op | source)
XLA Modules:
  0.0 84.9 jit_solution(10016415936027116678)
XLA Ops:
  1.3 78.6 %forward_solve.1 = (f32[768,1024]{1,0:T(8,128)}, f32[192,1024]{1,0:T(8,128)}) custom-call(s32[1]{0:T(128)S(6)} %copy.12.size_ref, s32[1,512]{1,0:T(1,128)} %bitcast.1, f32[768,1024]{1,0:T(8,128)} %rhs_hbm.1, f32[768,256]{1,0:T(8,128)} %lower_hbm.1, f32[768,768]{1,0:T(8,128)} %inverse_hbm.1, f32[512,768]{1,0:T(8,128)} %coupling_hbm.1, ...), custom_call_target="tpu_custom_call" | custom-call | tf_op jit(solution)/shard_map/forward_solve/pallas_call | solution.py:358
  79.9 0.0 copy-start
  79.9 4.0 %copy.13 = f32[768,1024]{1,0:T(8,128)} copy(f32[768,1024]{1,0:T(8,128)} %get-tuple-element.4) | data formatting | bytes 6291456
  84.0 0.0 copy-done
  84.0 0.9 %copy.14 = f32[192,1024]{1,0:T(8,128)} copy(f32[192,1024]{1,0:T(8,128)S(1)} %copy-done) | data formatting | bytes 1572864
Async XLA Ops:
  79.9 4.1 %copy-start = (f32[192,1024]{1,0:T(8,128)S(1)}, f32[192,1024]{1,0:T(8,128)}, u32[]{:S(2)}) copy-start(f32[192,1024]{1,0:T(8,128)} %get-tuple-element.5) | copy-start | bytes 2359300

commit v3 on v1

--- a/solution.py
+++ b/solution.py
@@ -155,6 +155,13 @@
         live = jnp.where(place < size, inverse[rows, :depth], 0.0)
         inv_high[rows, :depth], inv_low[rows, :depth] = split(live)
 
+    def send_on(turn):
+        @pl.when(jnp.logical_and(row == 0, turn < pairs))
+        def _():
+            pair = pair_of(turn)
+            chain_copy(2 * pair).start()
+            chain_copy(2 * pair + 1).start()
+
     loads[0].wait()
     prepare(0)
     loads[1].wait()
@@ -166,10 +173,9 @@
         high, low = split(rhs[pl.ds(0, TILE), cols])
         leaf[pl.ds(0, TILE), cols] = triangle(inv_high, inv_low, 0, high, low)
 
-        @pl.when(row == 0)
+        @pl.when(turn == 0)
         def _():
-            chain_copy(2 * pair).start()
-            chain_copy(2 * pair + 1).start()
+            send_on(0)
 
     for tile in range(1, tiles):
         prepare(tile)
@@ -180,6 +186,8 @@
         step = triangle(inv_high, inv_low, tile, lower_high, lower_low)
         step_high[rows, :], step_low[rows, :] = split(step)
     loads[3].wait()
+
+    send_on(1)
 
     @pl.loop(0, pairs)
     def _(turn):
@@ -224,6 +232,7 @@
                 rows = pl.ds(tile * TILE, TILE)
                 leaf[rows, cols] -= dot_split(step_high[rows, :], step_low[rows, :], high, low)
 
+        send_on(turn + 2)
         leaf_copy(pair).start()
         high, low = split(leaf[:, cols])
         for tile in range(anc_tiles):
@@ -262,6 +271,10 @@
             rows_of(shares, part, tile * TILE, share, result)
         for off in range(1, n_row):
             share_copy(part, off).start()
+
+    @pl.loop(0, owned)
+    def _(part):
+        mine = part * n_grid + grid
         own = shares[part, row]
         for off in range(1, n_row):
             share_copy(part, off).wait_recv()

time: 82.1 us -> 81.7 us (level)
  Pallas kernels: 75.7 us -> 74.5 us
    pallas_call x1, Pallas kernels: 75.7 us -> 74.5 us  [body(): pl.pallas_call(functools.partial(kernel, n_grid, n_row), out_shape=(jax.S...]
where the time goes in v3:
time: 81.7 us; the launch traced here: 80.7 us
  Pallas kernels  74.5 us (91%)
  local copies, waits for them, and re-layouts  4.93 us (6%)
  between operations  1.29 us (2%)
    pallas_call x1, Pallas kernels, body(): pl.pallas_call(functools.partial(kernel, n_grid, n_row), out_shape=(jax.S...  74.5 us
    unnamed x4, local copies, waits for them, and re-layouts  4.93 us

profile of v3, /device:TPU:0, one launch (start us, length us, event | category | flops | bytes accessed | tf_op | source)
XLA Modules:
  0.0 80.7 jit_solution(10110077697157829728)
XLA Ops:
  1.3 74.5 %forward_solve.1 = (f32[768,1024]{1,0:T(8,128)}, f32[192,1024]{1,0:T(8,128)}) custom-call(s32[1]{0:T(128)S(6)} %copy.12.size_ref, s32[1,512]{1,0:T(1,128)} %bitcast.1, f32[768,1024]{1,0:T(8,128)} %rhs_hbm.1, f32[768,256]{1,0:T(8,128)} %lower_hbm.1, f32[768,768]{1,0:T(8,128)} %inverse_hbm.1, f32[512,768]{1,0:T(8,128)} %coupling_hbm.1, ...), custom_call_target="tpu_custom_call" | custom-call | tf_op jit(solution)/shard_map/forward_solve/pallas_call | solution.py:335
  75.8 0.0 copy-start
  75.8 4.0 %copy.13 = f32[768,1024]{1,0:T(8,128)} copy(f32[768,1024]{1,0:T(8,128)} %get-tuple-element.4) | data formatting | bytes 6291456
  79.8 0.0 copy-done
  79.8 0.9 %copy.14 = f32[192,1024]{1,0:T(8,128)} copy(f32[192,1024]{1,0:T(8,128)S(1)} %copy-done) | data formatting | bytes 1572864
Async XLA Ops:
  75.8 4.1 %copy-start = (f32[192,1024]{1,0:T(8,128)S(1)}, f32[192,1024]{1,0:T(8,128)}, u32[]{:S(2)}) copy-start(f32[192,1024]{1,0:T(8,128)} %get-tuple-element.5) | copy-start | bytes 2359300

commit v4 on v3

--- a/solution.py
+++ b/solution.py
@@ -65,7 +65,7 @@
         return pl.ds(pl.multiple_of(pair * wide, wide), wide)
 
     def pair_of(turn):
-        return (turn // cycle) * cycle + lax.rem(lax.rem(turn, cycle) + grid // 2 + 1, cycle)
+        return lax.rem(turn, owned) * cycle + lax.rem(turn // owned + grid // 2 + 1, cycle)
 
     loads = [
         pltpu.make_async_copy(inverse_hbm, inverse, load_sem.at[0]),

time: 81.7 us -> 81.9 us (level)
  no operation moved by 1% of the time
where the time goes in v4:
time: 81.9 us; the launch traced here: 80.9 us
  Pallas kernels  74.7 us (91%)
  local copies, waits for them, and re-layouts  4.93 us (6%)
  between operations  1.29 us (2%)
    pallas_call x1, Pallas kernels, body(): pl.pallas_call(functools.partial(kernel, n_grid, n_row), out_shape=(jax.S...  74.7 us
    unnamed x4, local copies, waits for them, and re-layouts  4.93 us

profile of v4, /device:TPU:0, one launch (start us, length us, event | category | flops | bytes accessed | tf_op | source)
XLA Modules:
  0.0 80.9 jit_solution(18245610961491315589)
XLA Ops:
  1.3 74.7 %forward_solve.1 = (f32[768,1024]{1,0:T(8,128)}, f32[192,1024]{1,0:T(8,128)}) custom-call(s32[1]{0:T(128)S(6)} %copy.12.size_ref, s32[1,512]{1,0:T(1,128)} %bitcast.1, f32[768,1024]{1,0:T(8,128)} %rhs_hbm.1, f32[768,256]{1,0:T(8,128)} %lower_hbm.1, f32[768,768]{1,0:T(8,128)} %inverse_hbm.1, f32[512,768]{1,0:T(8,128)} %coupling_hbm.1, ...), custom_call_target="tpu_custom_call" | custom-call | tf_op jit(solution)/shard_map/forward_solve/pallas_call | solution.py:335
  76.0 0.0 copy-start
  76.0 4.0 %copy.13 = f32[768,1024]{1,0:T(8,128)} copy(f32[768,1024]{1,0:T(8,128)} %get-tuple-element.4) | data formatting | bytes 6291456
  80.0 0.0 copy-done
  80.0 0.9 %copy.14 = f32[192,1024]{1,0:T(8,128)} copy(f32[192,1024]{1,0:T(8,128)S(1)} %copy-done) | data formatting | bytes 1572864
Async XLA Ops:
  76.0 4.1 %copy-start = (f32[192,1024]{1,0:T(8,128)S(1)}, f32[192,1024]{1,0:T(8,128)}, u32[]{:S(2)}) copy-start(f32[192,1024]{1,0:T(8,128)} %get-tuple-element.5) | copy-start | bytes 2359300
